TPU v7x, 128 devices: a whole 4x4x4 slice. The times are simulated.
128 devices in a mesh: mom: 16 (over z, y), hist: 8 (over x, core).
Axes of the slice: x: 4, y: 4, z: 4, core: 2. Of those that a mesh axis runs over, the one named last changes fastest.
Arguments:
- greens: bfloat16 [2, 64, 1024, 1024], P(None, 'hist', 'mom'), may hold values from -6 to 6
- advanced: bfloat16 [2, 1024, 64, 1024], P(None, 'mom', 'hist'), may hold values from -1 to 1
- coupling: float32 [1024], P('mom'), may hold values from 0.3 to 1
- bounds: int32 [8], replicated, may hold values from 1 to 64, as said below
Outputs:
- collision: float32 [8, 2, 1024, 1024], P('hist', None, 'mom')
Inputs may be any that keep to these rules, and one draw needn't show every extreme that they name: `bounds`: every draw has some target time index whose memory covers all 64 stored steps.
All inputs are finite; a program needn't handle non-finite values.
Results may differ from a plain program's by a relative error of at most 0.012.
Values may be sent and summed in bfloat16 or wider, within the bound.
A program may use at most 128 MiB of HBM per device.

v0:
```python
import functools
import math

import jax
import jax.numpy as jnp
import ml_dtypes
import numpy as np
from jax import lax
from jax.experimental import pallas as pl
from jax.experimental.pallas import tpu as pltpu
from jax.sharding import PartitionSpec as P

MESH = pl.DeviceIdType.MESH
L = 32
NO = 32
LANES = 128
CHUNKS = 8
MOM = 16
HIST = 8
STEPS = 8
KDEV = 64
GROUPS = 4
AHEAD = 3
BACK = 2
LAST = 2


def tables():
    index = np.arange(L, dtype=np.int32)
    phase = index[:, None] * index[None, :] % L
    angle = phase.astype(np.float32) * np.float32(2.0 * math.pi / L)
    norm = np.float32(1.0 / math.sqrt(L))
    cosines = (np.cos(angle) * norm).astype(ml_dtypes.bfloat16).astype(np.float32)
    sines = (np.sin(angle) * norm).astype(ml_dtypes.bfloat16).astype(np.float32)
    ahead = np.array([[cosines, -sines], [sines, cosines]])
    back = np.array([[cosines, sines], [-sines, cosines]])
    eye = np.eye(2, dtype=np.float32)
    group = np.array([[0, 16]] + [[m, L - m] for m in range(1, MOM)])
    flip = (-index) % L
    pairs = np.arange(L).reshape(MOM, 2)

    first = np.einsum("ridyk,st,lm->dsyrlitmk", ahead[:, :, group, :].reshape(2, 2, MOM, 2, L), eye, eye)
    along = ahead[:, :, :, pairs]
    space = np.einsum("rixdl,st,yw->rsyxdtwil", along, eye, eye)
    turned = along[:, :, flip]
    mirror = np.einsum("rixdl,st,yw->rsyxdtwil", turned, eye, eye[::-1])
    mirror_own = np.einsum("rixdl,st,yw->rsyxdtwil", turned, eye, eye)
    third = np.einsum("ridlx,st,yw->dsyrlitwx", back[:, :, pairs, :], eye, eye)
    last = np.einsum("rikdy,st,lm->rslkdtyim", back[:, :, :, group], eye, eye)
    square = lambda a: a.reshape(256, 256)
    moved = [np.concatenate([square(space), square(m)]) for m in (mirror, mirror_own)]
    return (
        np.stack([square(first), square(third), square(last)]).astype(ml_dtypes.bfloat16),
        np.stack(moved).astype(ml_dtypes.bfloat16),
    )


def other(me, d):
    return lax.rem(me // 4 + d // 4, 4) * 4 + lax.rem(lax.rem(me, 4) + d % 4, 4)


def kernel(
    greens, advanced, coupling, bounds, tabs, space_tab, out,
    gbuf, abuf, tbuf, sbuf, bbuf, own_c, all_c, masks,
    s1, r1, s2, r2, rows, bt, at, acc, cs, cr, obuf,
    in_sem, load_sem, c_send, c_recv, s1_send, r1_recv, s2_send, r2_recv, cs_send, cr_recv, o_sem,
):
    me = lax.axis_index("mom")
    h = lax.axis_index("hist")

    def lanes(c):
        return pl.ds(pl.multiple_of(c * LANES, LANES), LANES)

    pick = jnp.where(me == 0, 1, 0)
    tab_copy = pltpu.make_async_copy(tabs, tbuf, load_sem.at[0])
    space_copy = pltpu.make_async_copy(space_tab.at[pick], sbuf, load_sem.at[1])
    adv_copy = pltpu.make_async_copy(advanced, abuf, load_sem.at[2])
    bound_copy = pltpu.make_async_copy(bounds, bbuf, load_sem.at[3])

    def green_copy(c):
        return pltpu.make_async_copy(greens.at[:, :, :, lanes(c)], gbuf.at[c], in_sem.at[c])

    tab_copy.start()
    green_copy(0).start()
    green_copy(1).start()
    space_copy.start()
    bound_copy.start()

    barrier = pltpu.get_barrier_semaphore()
    for d in range(1, MOM):
        pl.semaphore_signal(barrier, inc=1, device_id=(other(me, d), h), device_id_type=MESH)
    for d in range(1, HIST):
        pl.semaphore_signal(barrier, inc=1, device_id=(me, lax.rem(h + d, HIST)), device_id_type=MESH)

    for c in range(2, CHUNKS):
        green_copy(c).start()
    adv_copy.start()

    def exchange(src, dst, send, recv, c):
        for d in range(1, MOM):
            p = other(me, d)
            pltpu.make_async_remote_copy(
                src_ref=src.at[c, p], dst_ref=dst.at[c, me], send_sem=send.at[c], recv_sem=recv.at[c],
                device_id=(p, h), device_id_type=MESH,
            ).start()
        dst[c, me] = src[c, me]

    def arrivals(src, dst, send, recv, c):
        return pltpu.make_async_remote_copy(
            src_ref=src.at[c, pl.ds(0, MOM - 1)], dst_ref=dst.at[c, pl.ds(0, MOM - 1)],
            send_sem=send.at[c], recv_sem=recv.at[c], device_id=(other(me, 1), h), device_id_type=MESH,
        )

    def coupling_copy(p):
        return pltpu.make_async_remote_copy(
            src_ref=own_c, dst_ref=all_c.at[me], send_sem=c_send, recv_sem=c_recv,
            device_id=(p, h), device_id_type=MESH,
        )

    def coupling_all():
        return pltpu.make_async_remote_copy(
            src_ref=all_c.at[pl.ds(0, MOM - 1)], dst_ref=all_c.at[pl.ds(0, MOM - 1)], send_sem=c_send, recv_sem=c_recv,
            device_id=(other(me, 1), h), device_id_type=MESH,
        )

    def partial_all(c):
        return pltpu.make_async_remote_copy(
            src_ref=cs.at[c, pl.ds(0, HIST - 1)], dst_ref=cr.at[c, pl.ds(0, HIST - 1)],
            send_sem=cs_send.at[c], recv_sem=cr_recv.at[c], device_id=(me, lax.rem(h + 1, HIST)), device_id_type=MESH,
        )

    def two(load, q):
        return jnp.concatenate([load(2 * q), load(2 * q + 1)], axis=1)

    def spread(dst, c, q, value):
        value = value.astype(jnp.bfloat16)
        for n in range(2):
            part = value[:, n * LANES:(n + 1) * LANES].reshape(MOM, 16, LANES)
            dst[c, :, pl.ds((2 * q + n) * 16, 16), :] = part

    def gathered(src, c):
        return lambda g: src[c, :, pl.ds(g * 16, 16), :].reshape(256, LANES)

    def forward(c):
        green_copy(c).wait()
        for q in range(2):
            data = two(lambda g: gbuf[c, :, pl.ds(2 * g, 2)].reshape(256, LANES), q)
            spread(s1, c, q, jnp.dot(tbuf[0], data, preferred_element_type=jnp.float32))

    def middle(c):
        arrivals(s1, r1, s1_send, r1_recv, c).wait_recv()
        low = lax.broadcasted_iota(jnp.int32, (1, LANES), 1) < LANES // 2
        weight = jnp.where(low, all_c[2 * c, 0:1, :], all_c[2 * c + 1, 0:1, :])
        weight = weight * weight
        weight = jnp.concatenate([weight, weight], axis=1)
        for q in range(2):
            data = two(gathered(r1, c), q)
            space = jnp.dot(sbuf[...], data, preferred_element_type=jnp.float32)
            re, im, mre, mim = (space[n * 128:(n + 1) * 128] for n in range(4))
            square_re = re * re - im * im
            square_im = 2.0 * re * im
            sigma_re = weight * (square_re * mre + square_im * mim)
            sigma_im = weight * (square_im * mre - square_re * mim)
            sigma = jnp.concatenate([sigma_re.astype(jnp.bfloat16), sigma_im.astype(jnp.bfloat16)], axis=0)
            spread(s2, c, q, jnp.dot(tbuf[1], sigma, preferred_element_type=jnp.float32))

    def products(c):
        arrivals(s2, r2, s2_send, r2_recv, c).wait_recv()
        for q in range(2):
            final = jnp.dot(tbuf[2], two(gathered(r2, c), q), preferred_element_type=jnp.float32)
            for n in range(2):
                for part in range(2):
                    block = final[part * 128:(part + 1) * 128, n * LANES:(n + 1) * LANES]
                    at[2 * q + n, part] = block.T

        def one_group(g, carry):
            def one_orbital(m, sums):
                b_re = bt[g, 0, pl.ds(pl.multiple_of(m * NO, NO), NO), :]
                b_im = bt[g, 1, pl.ds(pl.multiple_of(m * NO, NO), NO), :]
                result = []
                for a in range(4):
                    a_re = at[g, 0, pl.ds(a * NO + m, 1), :]
                    a_im = at[g, 1, pl.ds(a * NO + m, 1), :]
                    result.append(sums[2 * a] + a_re * b_re - a_im * b_im)
                    result.append(sums[2 * a + 1] + a_re * b_im + a_im * b_re)
                return tuple(result)

            zero = jnp.zeros((NO, LANES), jnp.float32)
            sums = lax.fori_loop(0, NO, one_orbital, (zero,) * 8, unroll=4)
            for a in range(4):
                acc[g, 0, pl.ds(a * NO, NO), :] = sums[2 * a]
                acc[g, 1, pl.ds(a * NO, NO), :] = sums[2 * a + 1]
            return carry

        lax.fori_loop(0, GROUPS, one_group, 0)

        def one_target(j, carry):
            low = lax.broadcasted_iota(jnp.int32, (NO, LANES), 1) < LANES // 2
            for a in range(4):
                total_re = total_im = None
                for g in range(GROUPS):
                    mask = masks[j, g, 0:1, :]
                    term_re = acc[g, 0, pl.ds(a * NO, NO), :] * mask
                    term_im = acc[g, 1, pl.ds(a * NO, NO), :] * mask
                    total_re = term_re if g == 0 else total_re + term_re
                    total_im = term_im if g == 0 else total_im + term_im
                kept = jnp.where(low, total_re, total_im)
                moved = pltpu.roll(jnp.where(low, total_im, total_re), LANES // 2, 1)
                cs[c, j, pl.ds(a * NO, NO), :] = (kept + moved).astype(jnp.bfloat16)
            return carry

        lax.fori_loop(0, HIST, one_target, 0)
        for d in range(1, HIST):
            p = lax.rem(h + d, HIST)
            pltpu.make_async_remote_copy(
                src_ref=cs.at[c, p], dst_ref=cr.at[c, h], send_sem=cs_send.at[c], recv_sem=cr_recv.at[c],
                device_id=(me, p), device_id_type=MESH,
            ).start()

    def out_copy(c):
        return pltpu.make_async_copy(obuf.at[c], out.at[0, :, :, lanes(c)], o_sem.at[c])

    def finish(c):
        partial_all(c).wait_recv()
        total = cs[c, h].astype(jnp.float32)
        for d in range(1, HIST):
            total = total + cr[c, lax.rem(h + d, HIST)].astype(jnp.float32)
        obuf[c] = total.T.reshape(2, KDEV, LANES)
        out_copy(c).start()

    def prepare_masks():
        bound_copy.wait()
        half = lax.broadcasted_iota(jnp.int32, (8, LANES), 1) // (LANES // 2)
        for j in range(HIST):
            for g in range(GROUPS):
                step = h * STEPS + 2 * g + half
                masks[j, g] = jnp.where(step < bbuf[j], 1.0 / math.sqrt(STEPS * HIST), 0.0).astype(jnp.float32)

    def prepare_advanced():
        adv_copy.wait()

        def one(n, carry):
            part, t = n // CHUNKS, lax.rem(n, CHUNKS)
            block = abuf[part, :, :, lanes(t)].astype(jnp.float32)
            rows[...] = block.reshape(KDEV * STEPS, LANES)
            for g in range(GROUPS):
                square = jnp.concatenate([rows[pl.ds(2 * g + s, KDEV, STEPS), :] for s in range(2)], axis=0)
                bt[g, part, pl.ds(pl.multiple_of(t * LANES, LANES), LANES), :] = square.T
            return carry

        lax.fori_loop(0, 2 * CHUNKS, one, 0)

    pair = coupling[...].reshape(1, KDEV)
    own_c[...] = jnp.broadcast_to(jnp.concatenate([pair, pair], axis=1), (8, LANES))
    all_c[me] = own_c[...]
    tab_copy.wait()
    forward(0)
    pl.semaphore_wait(barrier, MOM - 1 + HIST - 1)
    for d in range(1, MOM):
        coupling_copy(other(me, d)).start()
    exchange(s1, r1, s1_send, r1_recv, 0)

    def send_ahead(c, carry):
        forward(c)
        exchange(s1, r1, s1_send, r1_recv, c)
        return carry

    lax.fori_loop(1, AHEAD, send_ahead, 0)
    prepare_masks()
    prepare_advanced()
    space_copy.wait()
    coupling_all().wait_recv()

    def step(i, carry):
        @pl.when(i < CHUNKS)
        def _():
            middle(i)
            exchange(s2, r2, s2_send, r2_recv, i)

        @pl.when(i + AHEAD < CHUNKS)
        def _():
            send_ahead(i + AHEAD, 0)

        @pl.when((i >= BACK) & (i < CHUNKS + BACK))
        def _():
            products(i - BACK)

        @pl.when(i >= BACK + LAST)
        def _():
            finish(i - BACK - LAST)

        return carry

    lax.fori_loop(0, CHUNKS + BACK + LAST, step, 0)

    def drain(c, carry):
        arrivals(s1, r1, s1_send, r1_recv, c).wait_send()
        arrivals(s2, r2, s2_send, r2_recv, c).wait_send()
        partial_all(c).wait_send()
        out_copy(c).wait()
        return carry

    coupling_all().wait_send()
    lax.fori_loop(0, CHUNKS, drain, 0)


def per_device(greens, advanced, coupling, bounds):
    tabs, space_tab = tables()
    any_spec = pl.BlockSpec(memory_space=pl.ANY)
    bf16, f32 = jnp.bfloat16, jnp.float32
    dma = pltpu.SemaphoreType.DMA
    blocks = pltpu.VMEM((CHUNKS, MOM, 64, LANES), bf16)
    parts = pltpu.VMEM((CHUNKS, HIST, LANES, LANES), bf16)
    return pl.pallas_call(
        kernel,
        out_shape=jax.ShapeDtypeStruct((1, 2, KDEV, NO * NO), f32),
        in_specs=[any_spec, any_spec, pl.BlockSpec(memory_space=pltpu.VMEM), any_spec, any_spec, any_spec],
        out_specs=any_spec,
        scratch_shapes=[
            pltpu.VMEM((CHUNKS, 2, STEPS, KDEV, LANES), bf16),
            pltpu.VMEM((2, KDEV, STEPS, NO * NO), bf16),
            pltpu.VMEM((3, 256, 256), bf16),
            pltpu.VMEM((512, 256), bf16),
            pltpu.SMEM((HIST,), jnp.int32),
            pltpu.VMEM((8, LANES), f32),
            pltpu.VMEM((MOM, 8, LANES), f32),
            pltpu.VMEM((HIST, GROUPS, 8, LANES), f32),
            blocks, blocks, blocks, blocks,
            pltpu.VMEM((KDEV * STEPS, LANES), f32),
            pltpu.VMEM((GROUPS, 2, NO * NO, LANES), f32),
            pltpu.VMEM((GROUPS, 2, LANES, LANES), f32),
            pltpu.VMEM((GROUPS, 2, LANES, LANES), f32),
            parts, parts,
            pltpu.VMEM((CHUNKS, 2, KDEV, LANES), f32),
            dma((CHUNKS,)), dma((4,)), dma, dma,
            dma((CHUNKS,)), dma((CHUNKS,)), dma((CHUNKS,)), dma((CHUNKS,)), dma((CHUNKS,)), dma((CHUNKS,)), dma((CHUNKS,)),
        ],
        compiler_params=pltpu.CompilerParams(collective_id=0, has_side_effects=True, vmem_limit_bytes=48 << 20),
    )(greens, advanced, coupling, bounds, jnp.asarray(tabs), jnp.asarray(space_tab))


def solution(mesh):
    in_specs = (P(None, "hist", "mom", None), P(None, "mom", "hist", None), P("mom"), P())
    out_specs = P("hist", None, "mom", None)
    return jax.shard_map(per_device, mesh=mesh, in_specs=in_specs, out_specs=out_specs, check_vma=False)
```

profile of v0, /device:TPU:1, one launch (start us, length us, event | category | flops | bytes accessed | tf_op | source)
XLA Modules:
  0.0 77.2 jit_solution(841839553638641960)
XLA Ops:
  0.0 0.0 copy-start
  0.0 1.6 %copy-done = bf16[2,8,64,1024]{3,2,1,0:T(8,128)(2,1)S(1)} copy-done((bf16[2,8,64,1024]{3,2,1,0:T(8,128)(2,1)S(1)}, bf16[2,8,64,1024]{3,2,1,0:T(8,128)(2,1)}, u32[]{:S(2)}) %copy-start) | copy-done | bytes 2097176
  1.6 0.0 copy-start.1
  1.6 1.6 %copy-done.1 = bf16[2,64,8,1024]{3,2,1,0:T(8,128)(2,1)S(1)} copy-done((bf16[2,64,8,1024]{3,2,1,0:T(8,128)(2,1)S(1)}, bf16[2,64,8,1024]{3,2,1,0:T(8,128)(2,1)}, u32[]{:S(2)}) %copy-start.1) | copy-done | bytes 2097176
  3.2 0.0 copy-start.2
  3.2 1.0 %copy-done.2 = bf16[2,512,256]{2,1,0:T(8,128)(2,1)S(1)} copy-done((bf16[2,512,256]{2,1,0:T(8,128)(2,1)S(1)}, bf16[2,512,256]{2,1,0:T(8,128)(2,1)}, u32[]{:S(2)}) %copy-start.2) | copy-done | bytes 524312
  4.2 0.0 copy-start.3
  4.2 1.0 %copy-done.3 = bf16[3,256,256]{2,1,0:T(8,128)(2,1)S(1)} copy-done((bf16[3,256,256]{2,1,0:T(8,128)(2,1)S(1)}, bf16[3,256,256]{2,1,0:T(8,128)(2,1)}, u32[]{:S(2)}) %copy-start.3) | copy-done | bytes 393240
  5.2 0.0 copy-start.4
  5.2 0.7 copy-done.4
  5.9 0.0 copy-start.5
  5.9 0.7 copy-done.5
  6.5 69.9 %shard_map.64 = f32[1,2,64,1024]{3,2,1,0:T(8,128)S(1)} custom-call(bf16[2,8,64,1024]{3,2,1,0:T(8,128)(2,1)S(1)} %copy-done, bf16[2,64,8,1024]{3,2,1,0:T(8,128)(2,1)S(1)} %copy-done.1, f32[64]{0:T(128)S(1)} %copy-done.4, s32[8]{0:T(128)S(1)} %copy-done.5, bf16[3,256,256]{2,1,0:T(8,128)(2,1)S(1)} %copy-done.3, bf16[2,512,256]{2,1,0:T(8,128)(2,1)S(1)} %copy-done.2), custom_call_target="tpu_custom_call" | custom-call | tf_op jit(solution)/shard_map/pallas_call | solution.py:314
  76.4 0.8 %copy.8 = f32[1,2,64,1024]{3,2,1,0:T(8,128)} copy(f32[1,2,64,1024]{3,2,1,0:T(8,128)S(1)} %shard_map.64) | data formatting | bytes 1048576
Async XLA Ops:
  0.0 1.6 %copy-start = (bf16[2,8,64,1024]{3,2,1,0:T(8,128)(2,1)S(1)}, bf16[2,8,64,1024]{3,2,1,0:T(8,128)(2,1)}, u32[]{:S(2)}) copy-start(bf16[2,8,64,1024]{3,2,1,0:T(8,128)(2,1)} %greens.1) | copy-start | bytes 6291460
  1.6 1.6 %copy-start.1 = (bf16[2,64,8,1024]{3,2,1,0:T(8,128)(2,1)S(1)}, bf16[2,64,8,1024]{3,2,1,0:T(8,128)(2,1)}, u32[]{:S(2)}) copy-start(bf16[2,64,8,1024]{3,2,1,0:T(8,128)(2,1)} %advanced.1) | copy-start | bytes 6291460
  3.2 1.0 %copy-start.2 = (bf16[2,512,256]{2,1,0:T(8,128)(2,1)S(1)}, bf16[2,512,256]{2,1,0:T(8,128)(2,1)}, u32[]{:S(2)}) copy-start(bf16[2,512,256]{2,1,0:T(8,128)(2,1)} %constant.5.clone.space_tab) | copy-start | bytes 1572868
  4.2 1.0 %copy-start.3 = (bf16[3,256,256]{2,1,0:T(8,128)(2,1)S(1)}, bf16[3,256,256]{2,1,0:T(8,128)(2,1)}, u32[]{:S(2)}) copy-start(bf16[3,256,256]{2,1,0:T(8,128)(2,1)} %constant.4.clone.tabs) | copy-start | bytes 1179652
  5.2 0.7 copy-start.4
  5.9 0.7 copy-start.5
where the time goes:
time: 77.5 us; the launch traced here: 77.2 us
  Pallas kernels  69.9 us (90%)
  local copies, waits for them, and re-layouts  7.32 us (9%)
    pallas_call x1, Pallas kernels, per_device(): pl.pallas_call(kernel, out_shape=jax.ShapeDtypeStruct((1, 2, KDEV, NO * N...  69.9 us
    unnamed x13, local copies, waits for them, and re-layouts  7.32 us

commit v1 on v0

v1 whole, which is shorter than its diff:
```python
import functools
import math

import jax
import jax.numpy as jnp
import ml_dtypes
import numpy as np
from jax import lax
from jax.experimental import pallas as pl
from jax.experimental.pallas import tpu as pltpu
from jax.sharding import PartitionSpec as P

MESH = pl.DeviceIdType.MESH
L = 32
NO = 32
LANES = 128
CHUNKS = 8
MOM = 16
HIST = 8
STEPS = 8
KDEV = 64
AHEAD = 3
BACK = 2
LAST = 2


def tables():
    index = np.arange(L, dtype=np.int32)
    phase = index[:, None] * index[None, :] % L
    angle = phase.astype(np.float32) * np.float32(2.0 * math.pi / L)
    norm = np.float32(1.0 / math.sqrt(L))
    cosines = (np.cos(angle) * norm).astype(ml_dtypes.bfloat16).astype(np.float32)
    sines = (np.sin(angle) * norm).astype(ml_dtypes.bfloat16).astype(np.float32)
    ahead = np.array([[cosines, -sines], [sines, cosines]])
    back = np.array([[cosines, sines], [-sines, cosines]])
    eye = np.eye(2, dtype=np.float32)
    group = np.array([[0, 16]] + [[m, L - m] for m in range(1, MOM)])
    flip = (-index) % L
    pairs = np.arange(L).reshape(MOM, 2)

    first = np.einsum("ridyk,st,lm->dsyrlitmk", ahead[:, :, group, :].reshape(2, 2, MOM, 2, L), eye, eye)
    along = ahead[:, :, :, pairs]
    space = np.einsum("rixdl,st,yw->rsyxdtwil", along, eye, eye)
    turned = along[:, :, flip]
    mirror = np.einsum("rixdl,st,yw->rsyxdtwil", turned, eye, eye[::-1])
    mirror_own = np.einsum("rixdl,st,yw->rsyxdtwil", turned, eye, eye)
    third = np.einsum("ridlx,st,yw->dlsyritwx", back[:, :, pairs, :], eye, eye)
    last = np.einsum("rikdy,st->rskdtyi", back[:, :, :, group], np.eye(4, dtype=np.float32))
    square = lambda a: a.reshape(256, 256)
    moved = [np.concatenate([square(space), square(m)]) for m in (mirror, mirror_own)]
    return (
        np.stack([square(first), square(third), square(last)]).astype(ml_dtypes.bfloat16),
        np.stack(moved).astype(ml_dtypes.bfloat16),
    )


def other(me, d):
    return lax.rem(me // 4 + d // 4, 4) * 4 + lax.rem(lax.rem(me, 4) + d % 4, 4)


def kernel(
    greens, advanced, coupling, bounds, tabs, space_tab, out,
    gbuf, abuf, tbuf, sbuf, bbuf, cbuf, own_c, all_c, masks,
    s1, r1, s2, r2, rows, bt, at, acc, cs, cr,
    in_sem, load_sem, c_send, c_recv, s1_send, r1_recv, s2_send, r2_recv, cs_send, cr_recv,
):
    me = lax.axis_index("mom")
    h = lax.axis_index("hist")

    def lanes(c):
        return pl.ds(pl.multiple_of(c * LANES, LANES), LANES)

    pick = jnp.where(me == 0, 1, 0)
    tab_copy = pltpu.make_async_copy(tabs, tbuf, load_sem.at[0])
    space_copy = pltpu.make_async_copy(space_tab.at[pick], sbuf, load_sem.at[1])
    adv_copy = pltpu.make_async_copy(advanced, abuf, load_sem.at[2])
    bound_copy = pltpu.make_async_copy(bounds, bbuf, load_sem.at[3])

    def green_copy(c):
        return pltpu.make_async_copy(greens.at[:, :, :, lanes(c)], gbuf.at[c], in_sem.at[c])

    coupling_load = pltpu.make_async_copy(coupling, cbuf, load_sem.at[4])
    coupling_load.start()
    tab_copy.start()
    green_copy(0).start()
    green_copy(1).start()
    space_copy.start()
    bound_copy.start()

    barrier = pltpu.get_barrier_semaphore()
    for d in range(1, MOM):
        pl.semaphore_signal(barrier, inc=1, device_id=(other(me, d), h), device_id_type=MESH)
    for d in range(1, HIST):
        pl.semaphore_signal(barrier, inc=1, device_id=(me, lax.rem(h + d, HIST)), device_id_type=MESH)

    for c in range(2, CHUNKS):
        green_copy(c).start()
    adv_copy.start()

    def exchange(src, dst, send, recv, c):
        for d in range(1, MOM):
            p = other(me, d)
            pltpu.make_async_remote_copy(
                src_ref=src.at[c, p], dst_ref=dst.at[c, me], send_sem=send.at[c], recv_sem=recv.at[c],
                device_id=(p, h), device_id_type=MESH,
            ).start()
        dst[c, me] = src[c, me]

    def arrivals(src, dst, send, recv, c):
        return pltpu.make_async_remote_copy(
            src_ref=src.at[c, pl.ds(0, MOM - 1)], dst_ref=dst.at[c, pl.ds(0, MOM - 1)],
            send_sem=send.at[c], recv_sem=recv.at[c], device_id=(other(me, 1), h), device_id_type=MESH,
        )

    def coupling_copy(p):
        return pltpu.make_async_remote_copy(
            src_ref=own_c, dst_ref=all_c.at[me], send_sem=c_send, recv_sem=c_recv,
            device_id=(p, h), device_id_type=MESH,
        )

    def coupling_all():
        return pltpu.make_async_remote_copy(
            src_ref=all_c.at[pl.ds(0, MOM - 1)], dst_ref=all_c.at[pl.ds(0, MOM - 1)], send_sem=c_send, recv_sem=c_recv,
            device_id=(other(me, 1), h), device_id_type=MESH,
        )

    def partial_all(c, low):
        return pltpu.make_async_remote_copy(
            src_ref=cs.at[c, low, pl.ds(0, HIST - 1)], dst_ref=cr.at[c, low, pl.ds(0, HIST - 1)],
            send_sem=cs_send.at[c, low], recv_sem=cr_recv.at[c, low], device_id=(me, lax.rem(h + 1, HIST)), device_id_type=MESH,
        )

    def two(load, q):
        return jnp.concatenate([load(2 * q), load(2 * q + 1)], axis=1)

    def spread(dst, c, q, value):
        value = value.astype(jnp.bfloat16)
        for n in range(2):
            part = value[:, n * LANES:(n + 1) * LANES].reshape(MOM, 16, LANES)
            dst[c, :, pl.ds((2 * q + n) * 16, 16), :] = part

    def gathered(src, c, first=0):
        return lambda g: src[c, :, pl.ds(first + g * 16, 16), :].reshape(256, LANES)

    def forward(c):
        green_copy(c).wait()
        for q in range(2):
            data = two(lambda g: gbuf[c, :, pl.ds(2 * g, 2)].reshape(256, LANES), q)
            spread(s1, c, q, jnp.dot(tbuf[0], data, preferred_element_type=jnp.float32))

    def middle(c):
        arrivals(s1, r1, s1_send, r1_recv, c).wait_recv()
        low = lax.broadcasted_iota(jnp.int32, (1, LANES), 1) < LANES // 2
        weight = jnp.where(low, all_c[2 * c, 0:1, :], all_c[2 * c + 1, 0:1, :])
        weight = weight * weight
        weight = jnp.concatenate([weight, weight], axis=1)
        for q in range(2):
            data = two(gathered(r1, c), q)
            space = jnp.dot(sbuf[...], data, preferred_element_type=jnp.float32)
            re, im, mre, mim = (space[n * 128:(n + 1) * 128] for n in range(4))
            square_re = re * re - im * im
            square_im = 2.0 * re * im
            sigma_re = weight * (square_re * mre + square_im * mim)
            sigma_im = weight * (square_im * mre - square_re * mim)
            sigma = jnp.concatenate([sigma_re.astype(jnp.bfloat16), sigma_im.astype(jnp.bfloat16)], axis=0)
            value = jnp.dot(tbuf[1], sigma, preferred_element_type=jnp.float32).reshape(MOM, 2, 8, 2 * LANES)
            value = jnp.concatenate([value[..., :LANES], value[..., LANES:]], axis=2).astype(jnp.bfloat16)
            for low in range(2):
                s2[c, :, pl.ds(low * 32 + q * 16, 16), :] = value[:, low]

    def products(c, low):
        final = jnp.dot(tbuf[2], two(gathered(r2, c, low * 32), 0), preferred_element_type=jnp.float32)
        for g in range(2):
            re = final[:128, g * LANES:(g + 1) * LANES].T
            im = final[128:, g * LANES:(g + 1) * LANES].T
            at[g, 0] = re
            at[g, 1] = im
            at[g, 2] = re + im

        def one_block(n, carry):
            g, first = n // 2, lax.rem(n, 2) * (2 * NO)

            def one_orbital(m, sums):
                b = [bt[low, g, part, pl.ds(pl.multiple_of(m * NO, NO), NO), :] for part in range(3)]
                result = []
                for a in range(2):
                    for part in range(3):
                        factor = at[g, part, pl.ds(first + a * NO + m, 1), :]
                        result.append(sums[3 * a + part] + factor * b[part])
                return tuple(result)

            zero = jnp.zeros((NO, LANES), jnp.float32)
            sums = lax.fori_loop(0, NO, one_orbital, (zero,) * 6, unroll=8)
            for a in range(2):
                re_re, im_im, both = sums[3 * a:3 * a + 3]
                spot = pl.ds(pl.multiple_of(first + a * NO, NO), NO)
                acc[g, 0, spot, :] = (re_re - im_im).astype(jnp.bfloat16)
                acc[g, 1, spot, :] = (both - (re_re + im_im)).astype(jnp.bfloat16)
            return carry

        lax.fori_loop(0, 4, one_block, 0)
        terms = jnp.concatenate([acc[g].reshape(2 * LANES, LANES) for g in range(2)], axis=1)
        sums = lax.dot_general(masks[...], terms, (((1,), (1,)), ((), ())), preferred_element_type=jnp.float32)
        cs[c, low] = sums.astype(jnp.bfloat16).reshape(HIST, 32, 2 * LANES)
        for d in range(1, HIST):
            p = lax.rem(h + d, HIST)
            pltpu.make_async_remote_copy(
                src_ref=cs.at[c, low, p], dst_ref=cr.at[c, low, h],
                send_sem=cs_send.at[c, low], recv_sem=cr_recv.at[c, low],
                device_id=(me, p), device_id_type=MESH,
            ).start()

    def finish(c):
        for low in range(2):
            partial_all(c, low).wait_recv()
            total = cs[c, low, h].astype(jnp.float32)
            for d in range(1, HIST):
                total = total + cr[c, low, lax.rem(h + d, HIST)].astype(jnp.float32)
            for part in range(2):
                out[0, part, pl.ds(low * 32, 32), lanes(c)] = total[:, part * LANES:(part + 1) * LANES]

    def prepare_masks():
        bound_copy.wait()
        row_ky = lax.broadcasted_iota(jnp.int32, (32, 256), 0)
        column = lax.broadcasted_iota(jnp.int32, (32, 256), 1)
        step = h * STEPS + column // 32
        for j in range(HIST):
            keep = (step < bbuf[j]) & (column % 32 == row_ky)
            masks[pl.ds(32 * j, 32), :] = jnp.where(keep, 1.0 / math.sqrt(STEPS * HIST), 0.0).astype(jnp.bfloat16)

    def prepare_advanced():
        adv_copy.wait()

        def one(t, carry):
            for part in range(2):
                rows[part] = abuf[part, :, :, lanes(t)].astype(jnp.float32).reshape(KDEV * STEPS, LANES)
            spot = pl.ds(pl.multiple_of(t * LANES, LANES), LANES)
            for low in range(2):
                for g in range(2):
                    pair = []
                    for part in range(2):
                        pieces = [rows[part, pl.ds(low * 256 + 4 * g + s, 32, STEPS), :] for s in range(4)]
                        pair.append(jnp.concatenate(pieces, axis=0).T)
                        bt[low, g, part, spot, :] = pair[part]
                    bt[low, g, 2, spot, :] = pair[0] + pair[1]
            return carry

        lax.fori_loop(0, CHUNKS, one, 0)

    coupling_load.wait()
    pair = cbuf[...].reshape(1, KDEV)
    own_c[...] = jnp.broadcast_to(jnp.concatenate([pair, pair], axis=1), (8, LANES))
    all_c[me] = own_c[...]
    tab_copy.wait()
    forward(0)
    pl.semaphore_wait(barrier, MOM - 1 + HIST - 1)
    for d in range(1, MOM):
        coupling_copy(other(me, d)).start()
    exchange(s1, r1, s1_send, r1_recv, 0)

    def send_ahead(c, carry):
        forward(c)
        exchange(s1, r1, s1_send, r1_recv, c)
        return carry

    lax.fori_loop(1, AHEAD, send_ahead, 0)
    prepare_masks()
    prepare_advanced()
    space_copy.wait()
    coupling_all().wait_recv()

    def step(i, carry):
        @pl.when(i < CHUNKS)
        def _():
            middle(i)
            exchange(s2, r2, s2_send, r2_recv, i)

        @pl.when(i + AHEAD < CHUNKS)
        def _():
            send_ahead(i + AHEAD, 0)

        @pl.when((i >= BACK) & (i < CHUNKS + BACK))
        def _():
            arrivals(s2, r2, s2_send, r2_recv, i - BACK).wait_recv()
            for low in range(2):
                products(i - BACK, low)

        @pl.when(i >= BACK + LAST)
        def _():
            finish(i - BACK - LAST)

        return carry

    lax.fori_loop(0, CHUNKS + BACK + LAST, step, 0)

    def drain(c, carry):
        arrivals(s1, r1, s1_send, r1_recv, c).wait_send()
        arrivals(s2, r2, s2_send, r2_recv, c).wait_send()
        for low in range(2):
            partial_all(c, low).wait_send()
        return carry

    coupling_all().wait_send()
    lax.fori_loop(0, CHUNKS, drain, 0)


def per_device(greens, advanced, coupling, bounds):
    tabs, space_tab = tables()
    any_spec = pl.BlockSpec(memory_space=pltpu.HBM)
    bf16, f32 = jnp.bfloat16, jnp.float32
    dma = pltpu.SemaphoreType.DMA
    blocks = pltpu.VMEM((CHUNKS, MOM, 64, LANES), bf16)
    parts = pltpu.VMEM((CHUNKS, 2, HIST, 32, 2 * LANES), bf16)
    return pl.pallas_call(
        kernel,
        out_shape=pltpu.VMEM((1, 2, KDEV, NO * NO), f32),
        in_specs=[any_spec] * 6,
        out_specs=pl.BlockSpec(memory_space=pltpu.VMEM),
        scratch_shapes=[
            pltpu.VMEM((CHUNKS, 2, STEPS, KDEV, LANES), bf16),
            pltpu.VMEM((2, KDEV, STEPS, NO * NO), bf16),
            pltpu.VMEM((3, 256, 256), bf16),
            pltpu.VMEM((512, 256), bf16),
            pltpu.SMEM((HIST,), jnp.int32),
            pltpu.VMEM((KDEV,), f32),
            pltpu.VMEM((8, LANES), f32),
            pltpu.VMEM((MOM, 8, LANES), f32),
            pltpu.VMEM((256, 256), bf16),
            blocks, blocks, blocks, blocks,
            pltpu.VMEM((2, KDEV * STEPS, LANES), f32),
            pltpu.VMEM((2, 2, 3, NO * NO, LANES), f32),
            pltpu.VMEM((2, 3, LANES, LANES), f32),
            pltpu.VMEM((2, 2, LANES, LANES), bf16),
            parts, parts,
            dma((CHUNKS,)), dma((5,)), dma, dma,
            dma((CHUNKS,)), dma((CHUNKS,)), dma((CHUNKS,)), dma((CHUNKS,)), dma((CHUNKS, 2)), dma((CHUNKS, 2)),
        ],
        compiler_params=pltpu.CompilerParams(collective_id=0, has_side_effects=True, vmem_limit_bytes=63 << 20),
    )(greens, advanced, coupling, bounds, jnp.asarray(tabs), jnp.asarray(space_tab))


def solution(mesh):
    in_specs = (P(None, "hist", "mom", None), P(None, "mom", "hist", None), P("mom"), P())
    out_specs = P("hist", None, "mom", None)
    return jax.shard_map(per_device, mesh=mesh, in_specs=in_specs, out_specs=out_specs, check_vma=False)
```

time: 77.5 us -> 68.1 us (0.88)
  local copies, waits for them, and re-layouts: 7.32 us -> 0.8 us
  Pallas kernels: 69.9 us -> 67.2 us
    unnamed x13 -> x1, local copies, waits for them, and re-layouts: 7.32 us -> 0.8 us
    pallas_call x1, Pallas kernels: 69.9 us -> 67.2 us  [per_device(): pl.pallas_call(kernel, out_shape=pltpu.VMEM((1, 2, KDEV, NO * NO), f32),...]
where the time goes in v1:
time: 68.1 us; the launch traced here: 68 us
  Pallas kernels  67.2 us (99%)
  local copies, waits for them, and re-layouts  0.8 us (1%)
    pallas_call x1, Pallas kernels, per_device(): pl.pallas_call(kernel, out_shape=pltpu.VMEM((1, 2, KDEV, NO * NO), f32),...  67.2 us

profile of v1, /device:TPU:1, one launch (start us, length us, event | category | flops | bytes accessed | tf_op | source)
XLA Modules:
  0.0 68.0 jit_solution(6160553048936816949)
XLA Ops:
  0.0 67.2 %shard_map.64 = f32[1,2,64,1024]{3,2,1,0:T(8,128)S(1)} custom-call(bf16[2,8,64,1024]{3,2,1,0:T(8,128)(2,1)} %greens.1, bf16[2,64,8,1024]{3,2,1,0:T(8,128)(2,1)} %advanced.1, f32[64]{0:T(128)} %coupling.1, s32[8]{0:T(128)} %bounds.1, bf16[3,256,256]{2,1,0:T(8,128)(2,1)} %constant.4.clone.tabs, bf16[2,512,256]{2,1,0:T(8,128)(2,1)} %constant.5.clone.space_tab), custom_call_target="tpu_custom_call" | custom-call | tf_op jit(solution)/shard_map/pallas_call | solution.py:314
  67.2 0.8 %copy.8 = f32[1,2,64,1024]{3,2,1,0:T(8,128)} copy(f32[1,2,64,1024]{3,2,1,0:T(8,128)S(1)} %shard_map.64) | data formatting | bytes 1048576

commit v2 on v1

--- a/solution.py
+++ b/solution.py
@@ -79,6 +79,12 @@
     def green_copy(c):
         return pltpu.make_async_copy(greens.at[:, :, :, lanes(c)], gbuf.at[c], in_sem.at[c])
 
+    barrier = pltpu.get_barrier_semaphore()
+    for d in range(1, MOM):
+        pl.semaphore_signal(barrier, inc=1, device_id=(other(me, d), h), device_id_type=MESH)
+    for d in range(1, HIST):
+        pl.semaphore_signal(barrier, inc=1, device_id=(me, lax.rem(h + d, HIST)), device_id_type=MESH)
+
     coupling_load = pltpu.make_async_copy(coupling, cbuf, load_sem.at[4])
     coupling_load.start()
     tab_copy.start()
@@ -86,12 +92,6 @@
     green_copy(1).start()
     space_copy.start()
     bound_copy.start()
-
-    barrier = pltpu.get_barrier_semaphore()
-    for d in range(1, MOM):
-        pl.semaphore_signal(barrier, inc=1, device_id=(other(me, d), h), device_id_type=MESH)
-    for d in range(1, HIST):
-        pl.semaphore_signal(barrier, inc=1, device_id=(me, lax.rem(h + d, HIST)), device_id_type=MESH)
 
     for c in range(2, CHUNKS):
         green_copy(c).start()
@@ -105,6 +105,25 @@
                 device_id=(p, h), device_id_type=MESH,
             ).start()
         dst[c, me] = src[c, me]
+
+    def exchange_back(c):
+        for low in range(2):
+            half = pl.ds(low * 32, 32)
+            for d in range(1, MOM):
+                p = other(me, d)
+                pltpu.make_async_remote_copy(
+                    src_ref=s2.at[c, p, half], dst_ref=r2.at[c, me, half],
+                    send_sem=s2_send.at[c], recv_sem=r2_recv.at[c, low],
+                    device_id=(p, h), device_id_type=MESH,
+                ).start()
+        r2[c, me] = s2[c, me]
+
+    def arrivals_back(c, low):
+        half = pl.ds(low * 32, 32)
+        return pltpu.make_async_remote_copy(
+            src_ref=s2.at[c, pl.ds(0, MOM - 1), half], dst_ref=r2.at[c, pl.ds(0, MOM - 1), half],
+            send_sem=s2_send.at[c], recv_sem=r2_recv.at[c, low], device_id=(other(me, 1), h), device_id_type=MESH,
+        )
 
     def arrivals(src, dst, send, recv, c):
         return pltpu.make_async_remote_copy(
@@ -178,7 +197,7 @@
             at[g, 2] = re + im
 
         def one_block(n, carry):
-            g, first = n // 2, lax.rem(n, 2) * (2 * NO)
+            g, first = n // 2, n % 2 * (2 * NO)
 
             def one_orbital(m, sums):
                 b = [bt[low, g, part, pl.ds(pl.multiple_of(m * NO, NO), NO), :] for part in range(3)]
@@ -190,19 +209,20 @@
                 return tuple(result)
 
             zero = jnp.zeros((NO, LANES), jnp.float32)
-            sums = lax.fori_loop(0, NO, one_orbital, (zero,) * 6, unroll=8)
+            sums = lax.fori_loop(0, NO, one_orbital, (zero,) * 6, unroll=32)
             for a in range(2):
                 re_re, im_im, both = sums[3 * a:3 * a + 3]
-                spot = pl.ds(pl.multiple_of(first + a * NO, NO), NO)
+                spot = pl.ds(first + a * NO, NO)
                 acc[g, 0, spot, :] = (re_re - im_im).astype(jnp.bfloat16)
                 acc[g, 1, spot, :] = (both - (re_re + im_im)).astype(jnp.bfloat16)
             return carry
 
-        lax.fori_loop(0, 4, one_block, 0)
+        for n in range(4):
+            one_block(n, 0)
         terms = jnp.concatenate([acc[g].reshape(2 * LANES, LANES) for g in range(2)], axis=1)
         sums = lax.dot_general(masks[...], terms, (((1,), (1,)), ((), ())), preferred_element_type=jnp.float32)
         cs[c, low] = sums.astype(jnp.bfloat16).reshape(HIST, 32, 2 * LANES)
-        for d in range(1, HIST):
+        for d in (4, 5, 3, 2, 6, 7, 1):
             p = lax.rem(h + d, HIST)
             pltpu.make_async_remote_copy(
                 src_ref=cs.at[c, low, p], dst_ref=cr.at[c, low, h],
@@ -254,9 +274,9 @@
     tab_copy.wait()
     forward(0)
     pl.semaphore_wait(barrier, MOM - 1 + HIST - 1)
+    exchange(s1, r1, s1_send, r1_recv, 0)
     for d in range(1, MOM):
         coupling_copy(other(me, d)).start()
-    exchange(s1, r1, s1_send, r1_recv, 0)
 
     def send_ahead(c, carry):
         forward(c)
@@ -273,7 +293,7 @@
         @pl.when(i < CHUNKS)
         def _():
             middle(i)
-            exchange(s2, r2, s2_send, r2_recv, i)
+            exchange_back(i)
 
         @pl.when(i + AHEAD < CHUNKS)
         def _():
@@ -281,8 +301,8 @@
 
         @pl.when((i >= BACK) & (i < CHUNKS + BACK))
         def _():
-            arrivals(s2, r2, s2_send, r2_recv, i - BACK).wait_recv()
             for low in range(2):
+                arrivals_back(i - BACK, low).wait_recv()
                 products(i - BACK, low)
 
         @pl.when(i >= BACK + LAST)
@@ -295,7 +315,8 @@
 
     def drain(c, carry):
         arrivals(s1, r1, s1_send, r1_recv, c).wait_send()
-        arrivals(s2, r2, s2_send, r2_recv, c).wait_send()
+        for low in range(2):
+            arrivals_back(c, low).wait_send()
         for low in range(2):
             partial_all(c, low).wait_send()
         return carry
@@ -333,7 +354,7 @@
             pltpu.VMEM((2, 2, LANES, LANES), bf16),
             parts, parts,
             dma((CHUNKS,)), dma((5,)), dma, dma,
-            dma((CHUNKS,)), dma((CHUNKS,)), dma((CHUNKS,)), dma((CHUNKS,)), dma((CHUNKS, 2)), dma((CHUNKS, 2)),
+            dma((CHUNKS,)), dma((CHUNKS,)), dma((CHUNKS,)), dma((CHUNKS, 2)), dma((CHUNKS, 2)), dma((CHUNKS, 2)),
         ],
         compiler_params=pltpu.CompilerParams(collective_id=0, has_side_effects=True, vmem_limit_bytes=63 << 20),
     )(greens, advanced, coupling, bounds, jnp.asarray(tabs), jnp.asarray(space_tab))

time: 68.1 us -> 65.3 us (0.959)
  Pallas kernels: 67.2 us -> 64.4 us
    pallas_call x1, Pallas kernels: 67.2 us -> 64.4 us  [per_device(): pl.pallas_call(kernel, out_shape=pltpu.VMEM((1, 2, KDEV, NO * NO), f32),...]
where the time goes in v2:
time: 65.3 us; the launch traced here: 65.2 us
  Pallas kernels  64.4 us (99%)
  local copies, waits for them, and re-layouts  0.8 us (1%)
    pallas_call x1, Pallas kernels, per_device(): pl.pallas_call(kernel, out_shape=pltpu.VMEM((1, 2, KDEV, NO * NO), f32),...  64.4 us

profile of v2, /device:TPU:1, one launch (start us, length us, event | category | flops | bytes accessed | tf_op | source)
XLA Modules:
  0.0 65.2 jit_solution(7038378289294269937)
XLA Ops:
  0.0 64.4 %shard_map.64 = f32[1,2,64,1024]{3,2,1,0:T(8,128)S(1)} custom-call(bf16[2,8,64,1024]{3,2,1,0:T(8,128)(2,1)} %greens.1, bf16[2,64,8,1024]{3,2,1,0:T(8,128)(2,1)} %advanced.1, f32[64]{0:T(128)} %coupling.1, s32[8]{0:T(128)} %bounds.1, bf16[3,256,256]{2,1,0:T(8,128)(2,1)} %constant.4.clone.tabs, bf16[2,512,256]{2,1,0:T(8,128)(2,1)} %constant.5.clone.space_tab), custom_call_target="tpu_custom_call" | custom-call | tf_op jit(solution)/shard_map/pallas_call | solution.py:335
  64.4 0.8 %copy.8 = f32[1,2,64,1024]{3,2,1,0:T(8,128)} copy(f32[1,2,64,1024]{3,2,1,0:T(8,128)S(1)} %shard_map.64) | data formatting | bytes 1048576

commit v3 on v2

--- a/solution.py
+++ b/solution.py
@@ -19,8 +19,8 @@
 HIST = 8
 STEPS = 8
 KDEV = 64
-AHEAD = 3
-BACK = 2
+AHEAD = 4
+BACK = 3
 LAST = 2
 
 

time: 65.3 us -> 64.9 us (level)
  no operation moved by 1% of the time
where the time goes in v3:
time: 64.9 us; the launch traced here: 64.8 us
  Pallas kernels  64 us (99%)
  local copies, waits for them, and re-layouts  0.8 us (1%)
    pallas_call x1, Pallas kernels, per_device(): pl.pallas_call(kernel, out_shape=pltpu.VMEM((1, 2, KDEV, NO * NO), f32),...  64 us

profile of v3, /device:TPU:1, one launch (start us, length us, event | category | flops | bytes accessed | tf_op | source)
XLA Modules:
  0.0 64.8 jit_solution(8068823708940638510)
XLA Ops:
  0.0 64.0 %shard_map.64 = f32[1,2,64,1024]{3,2,1,0:T(8,128)S(1)} custom-call(bf16[2,8,64,1024]{3,2,1,0:T(8,128)(2,1)} %greens.1, bf16[2,64,8,1024]{3,2,1,0:T(8,128)(2,1)} %advanced.1, f32[64]{0:T(128)} %coupling.1, s32[8]{0:T(128)} %bounds.1, bf16[3,256,256]{2,1,0:T(8,128)(2,1)} %constant.4.clone.tabs, bf16[2,512,256]{2,1,0:T(8,128)(2,1)} %constant.5.clone.space_tab), custom_call_target="tpu_custom_call" | custom-call | tf_op jit(solution)/shard_map/pallas_call | solution.py:335
  64.0 0.8 %copy.8 = f32[1,2,64,1024]{3,2,1,0:T(8,128)} copy(f32[1,2,64,1024]{3,2,1,0:T(8,128)S(1)} %shard_map.64) | data formatting | bytes 1048576

commit v4 on v3

--- a/solution.py
+++ b/solution.py
@@ -253,7 +253,7 @@
 
         def one(t, carry):
             for part in range(2):
-                rows[part] = abuf[part, :, :, lanes(t)].astype(jnp.float32).reshape(KDEV * STEPS, LANES)
+                rows[part, pl.ds(0, KDEV * STEPS), :] = abuf[part, :, :, lanes(t)].astype(jnp.float32).reshape(KDEV * STEPS, LANES)
             spot = pl.ds(pl.multiple_of(t * LANES, LANES), LANES)
             for low in range(2):
                 for g in range(2):
@@ -348,7 +348,7 @@
             pltpu.VMEM((MOM, 8, LANES), f32),
             pltpu.VMEM((256, 256), bf16),
             blocks, blocks, blocks, blocks,
-            pltpu.VMEM((2, KDEV * STEPS, LANES), f32),
+            pltpu.VMEM((2, KDEV * STEPS + 8, LANES), f32),
             pltpu.VMEM((2, 2, 3, NO * NO, LANES), f32),
             pltpu.VMEM((2, 3, LANES, LANES), f32),
             pltpu.VMEM((2, 2, LANES, LANES), bf16),

time: 64.9 us -> 64.9 us (level)
  no operation moved by 1% of the time
where the time goes in v4:
time: 64.9 us; the launch traced here: 64.8 us
  Pallas kernels  64 us (99%)
  local copies, waits for them, and re-layouts  0.8 us (1%)
    pallas_call x1, Pallas kernels, per_device(): pl.pallas_call(kernel, out_shape=pltpu.VMEM((1, 2, KDEV, NO * NO), f32),...  64 us

profile of v4, /device:TPU:1, one launch (start us, length us, event | category | flops | bytes accessed | tf_op | source)
XLA Modules:
  0.0 64.8 jit_solution(6182297967946297381)
XLA Ops:
  0.0 64.0 %shard_map.64 = f32[1,2,64,1024]{3,2,1,0:T(8,128)S(1)} custom-call(bf16[2,8,64,1024]{3,2,1,0:T(8,128)(2,1)} %greens.1, bf16[2,64,8,1024]{3,2,1,0:T(8,128)(2,1)} %advanced.1, f32[64]{0:T(128)} %coupling.1, s32[8]{0:T(128)} %bounds.1, bf16[3,256,256]{2,1,0:T(8,128)(2,1)} %constant.4.clone.tabs, bf16[2,512,256]{2,1,0:T(8,128)(2,1)} %constant.5.clone.space_tab), custom_call_target="tpu_custom_call" | custom-call | tf_op jit(solution)/shard_map/pallas_call | solution.py:335
  64.0 0.8 %copy.8 = f32[1,2,64,1024]{3,2,1,0:T(8,128)} copy(f32[1,2,64,1024]{3,2,1,0:T(8,128)S(1)} %shard_map.64) | data formatting | bytes 1048576
